TPU v7x, 32 devices: a whole 2x2x4 slice. The times are simulated.
32 devices in a mesh: sample: 8 (over z, y), variant: 4 (over x, core).
Axes of the slice: x: 2, y: 2, z: 4, core: 2. Of those that a mesh axis runs over, the one named last changes fastest.
Arguments:
- dosage: bfloat16 [4096, 2048], P('sample', 'variant'), may hold values from 0 to 2
- covariates: float32 [30, 4096], P(None, 'sample'), may hold values from -6 to 6
- reach: int32 [4], replicated, may hold values from 1 to 2, as said below
Outputs:
- ld_bands: bfloat16 [4, 2048, 512], P(None, ('variant', 'sample'))
Inputs may be any that keep to these rules, and one draw needn't show every extreme that they name: `reach`: every draw has a block whose band reaches 2 blocks on each side.
All inputs are finite; a program needn't handle non-finite values.
Results may differ from a plain program's by a relative error of at most 0.015.
Values may be sent and summed in bfloat16 or wider, within the bound.
A program may use at most 64 MiB of HBM per device.

v0:
```python
import math

import jax
import jax.numpy as jnp
from jax import lax
from jax.sharding import PartitionSpec as P

MAXR = 2


def passed_along(block, axis, distance):
    devices = range(lax.axis_size(axis))
    route = [((i - distance) % len(devices), i) for i in devices]
    return lax.ppermute(block, axis, route)


def step_ahead(blocks):
    return passed_along(blocks, "variant", -1)


def shards(dosage, covariates, reach):
    highest = lax.Precision.HIGHEST
    local_samples = dosage.shape[0]
    samples = local_samples * lax.axis_size("sample")
    design = jnp.concatenate([jnp.ones((1, local_samples), jnp.float32), covariates], 0)
    genotype = dosage.astype(jnp.float32)
    moment_local = jnp.dot(design, design.T, precision=highest)
    cross_local = jnp.dot(design, genotype, precision=highest)
    moment, cross = lax.psum((moment_local, cross_local), "sample")
    factor = jnp.linalg.cholesky(moment)
    coefficients = jax.scipy.linalg.cho_solve((factor, True), cross)
    residual = genotype - jnp.dot(design.T, coefficients, precision=highest)
    spread = lax.psum(jnp.sum(residual * residual, 0), "sample")
    scaled = (residual * jnp.sqrt(samples / spread)).astype(jnp.bfloat16)
    own_reach = reach[lax.axis_index("variant")]
    inverse_root = 1.0 / math.sqrt(samples)
    slots = [None] * (2 * MAXR)
    ahead = scaled
    for offset in range(1, MAXR + 1):
        ahead = step_ahead(ahead)
        partial_tile = (
            lax.dot_general(
                scaled, ahead, (((0,), (0,)), ((), ())), preferred_element_type=jnp.float32
            )
            * inverse_root
        )
        finished = lax.psum_scatter(
            partial_tile.astype(jnp.bfloat16), "sample", scatter_dimension=0, tiled=True
        )
        slots[MAXR + offset - 1] = jnp.where(offset <= own_reach, finished, 0.0)
        swapped = lax.all_to_all(finished, "sample", split_axis=1, concat_axis=0, tiled=True)
        arrived = passed_along(swapped, "variant", offset).T
        slots[MAXR - offset] = jnp.where(offset <= own_reach, arrived, 0.0)
    return jnp.stack(slots)


def solution(mesh):
    placed = (P("sample", "variant"), P(None, "sample"), P())
    return jax.shard_map(
        shards,
        mesh=mesh,
        in_specs=placed,
        out_specs=P(None, ("variant", "sample"), None),
        check_vma=False,
    )
```

profile of v0, /device:TPU:0, one launch (start us, length us, event | category | flops | bytes accessed | tf_op | source)
XLA Modules:
  0.0 268.7 jit_solution(16767114878112964219)
XLA Ops:
  6.5 0.0 copy-start.1
  6.5 0.0 all-reduce.4.cloned.1.call-start
  6.5 1.7 fusion.5
  8.3 0.0 copy-done.1
  8.3 0.0 copy-start
  8.3 2.1 fusion.3
  10.4 0.0 all-reduce.4.cloned.1.call-update
  10.4 0.0 reduce-scatter.5.cloned.1.call-start
  10.5 72.0 %all-reduce.4.cloned.1.call-done = (f32[31,512]{1,0:T(8,128)}, f32[31,31]{0,1:T(8,128)}) async-done(((f32[31,512]{1,0:T(8,128)}, f32[31,31]{0,1:T(8,128)}), (f32[31,512]{1,0:T(8,128)}, f32[31,31]{0,1:T(8,128)})) %all-reduce.4.cloned.1.call-update) | async-done | bytes 67348 | tf_op jit(solution)/shard_map/psum | solution.py:29
  82.5 0.0 copy-start.4
  82.5 0.0 copy-start.5
  82.5 0.9 copy.9
  83.3 0.0 copy-done.4
  83.4 2.8 %cholesky.16 = f32[31,31]{1,0:T(8,128)S(1)} custom-call(f32[31,31]{1,0:T(8,128)S(1)} %fusion.12), custom_call_target="Cholesky" | custom-call | tf_op jit(solution)/shard_map/jit(cholesky)/cholesky | solution.py:30
  86.2 0.6 compare_reduce_fusion
  86.9 0.7 fusion.7
  87.5 2.4 custom-call.10
  89.9 0.0 copy-done.5
  89.9 0.3 fusion.10
  90.2 0.2 fusion.8
  90.4 0.0 copy-done
  90.4 1.1 multiply_reduce_fusion
  91.5 20.2 %psum.23 = f32[512]{0:T(512)S(1)} all-reduce(f32[512]{0:T(512)S(1)} %get-tuple-element.7), channel_id=1, replica_groups=mesh['sample'=8,'variant'=4] {'sample'}, use_global_device_ids=true, to_apply=%region_5.6 | all-reduce | flops 512 | bytes 4096 | tf_op jit(solution)/shard_map/psum | solution.py:33
  111.7 0.1 multiply_convert_fusion
  111.9 0.1 collective-permute-start
  111.9 6.7 %collective-permute-done = bf16[512,512]{1,0:T(8,128)(2,1)S(1)} collective-permute-done((bf16[512,512]{1,0:T(8,128)(2,1)S(1)}, bf16[512,512]{1,0:T(8,128)(2,1)S(1)}, u32[]{:S(2)}, u32[]{:S(2)}) %collective-permute-start) | collective-permute-done | bytes 524320 | tf_op jit(solution)/shard_map/ppermute | solution.py:14
  118.6 1.3 fusion.1
  119.9 0.0 reduce-scatter.5.cloned.1.call-update
  119.9 0.0 reduce-scatter.3.cloned.1.call-start
  120.0 2.0 collective-permute-start.1
  121.9 6.7 %collective-permute-done.1 = bf16[512,512]{1,0:T(8,128)(2,1)S(1)} collective-permute-done((bf16[512,512]{1,0:T(8,128)(2,1)S(1)}, bf16[512,512]{1,0:T(8,128)(2,1)S(1)}, u32[]{:S(2)}, u32[]{:S(2)}) %collective-permute-start.1) | collective-permute-done | bytes 524320 | tf_op jit(solution)/shard_map/ppermute | solution.py:14
  128.6 1.3 fusion
  129.9 0.0 reduce-scatter.3.cloned.1.call-update
  129.9 49.8 %reduce-scatter.5.cloned.1.call-done = bf16[64,512]{1,0:T(8,128)(2,1)} async-done(((bf16[512,512]{1,0:T(8,128)(2,1)}), bf16[64,512]{1,0:T(8,128)(2,1)}) %reduce-scatter.5.cloned.1.call-update) | async-done | bytes 65552 | tf_op jit(solution)/shard_map/reduce_scatter | solution.py:47
  179.7 1.0 all_to_all.32
  180.7 0.8 reshape.24
  181.5 3.6 %all-to-all-start.1 = ((bf16[8,2,2048]{2,1,0:T(2,128)(2,1)}), bf16[8,2,2048]{2,1,0:T(2,128)(2,1)S(1)}, u32[]{:S(2)}, u32[]{:S(2)}) async-start(bf16[8,2,2048]{2,1,0:T(2,128)(2,1)} %reshape.24), calls=%async_computation.3 | async-start | bytes 131072 | tf_op jit(solution)/shard_map/all_to_all | solution.py:51
  185.1 0.0 copy-start.6
  185.1 0.7 copy-done.6
  185.7 0.6 dynamic_slice.3
  187.6 4.4 %all-to-all-done.1 = bf16[8,2,2048]{2,1,0:T(2,128)(2,1)S(1)} async-done(((bf16[8,2,2048]{2,1,0:T(2,128)(2,1)}), bf16[8,2,2048]{2,1,0:T(2,128)(2,1)S(1)}, u32[]{:S(2)}, u32[]{:S(2)}) %all-to-all-start.1) | async-done | bytes 65568 | tf_op jit(solution)/shard_map/all_to_all | solution.py:51
  192.0 0.1 reshape.25
  192.1 0.0 copy-start.3
  192.1 0.1 copy.16
  192.2 0.1 collective-permute-start.3
  192.3 0.7 copy-done.3
  193.0 51.3 %reduce-scatter.3.cloned.1.call-done = bf16[64,512]{1,0:T(8,128)(2,1)} async-done(((bf16[512,512]{1,0:T(8,128)(2,1)}), bf16[64,512]{1,0:T(8,128)(2,1)}) %reduce-scatter.3.cloned.1.call-update) | async-done | bytes 65552 | tf_op jit(solution)/shard_map/reduce_scatter | solution.py:47
  244.3 1.0 copy.15
  245.3 0.8 reshape.26
  246.1 3.7 %all-to-all-start = ((bf16[8,2,2048]{2,1,0:T(2,128)(2,1)}), bf16[8,2,2048]{2,1,0:T(2,128)(2,1)S(1)}, u32[]{:S(2)}, u32[]{:S(2)}) async-start(bf16[8,2,2048]{2,1,0:T(2,128)(2,1)} %reshape.26), calls=%async_computation.1 | async-start | bytes 131072 | tf_op jit(solution)/shard_map/all_to_all | solution.py:51
  249.7 0.0 collective-permute-done.3
  249.8 6.9 %all-to-all-done = bf16[8,2,2048]{2,1,0:T(2,128)(2,1)S(1)} async-done(((bf16[8,2,2048]{2,1,0:T(2,128)(2,1)}), bf16[8,2,2048]{2,1,0:T(2,128)(2,1)S(1)}, u32[]{:S(2)}, u32[]{:S(2)}) %all-to-all-start) | async-done | bytes 65568 | tf_op jit(solution)/shard_map/all_to_all | solution.py:51
  256.6 0.1 reshape.27
  256.8 0.1 copy.11
  256.9 0.0 copy-start.2
  256.9 0.1 all_to_all.31
  257.1 1.5 collective-permute-start.2
  258.6 0.0 copy-done.2
  258.6 2.8 %collective-permute-done.2 = bf16[512,64]{0,1:T(8,128)(2,1)S(1)} collective-permute-done((bf16[512,64]{0,1:T(8,128)(2,1)S(1)}, bf16[512,64]{0,1:T(8,128)(2,1)S(1)}, u32[]{:S(2)}, u32[]{:S(2)}) %collective-permute-start.2) | collective-permute-done | bytes 65568 | tf_op jit(solution)/shard_map/ppermute | solution.py:14
  261.4 0.7 pad_maximum_fusion
  (9 shorter events, 0.1 us)
Async XLA Ops:
  6.5 1.8 copy-start.1
  6.5 75.9 %all-reduce.4.cloned.1.call-start = ((), (), s32[]{:S(2)}) async-start(), calls=%async_computation.6 | async-start | bytes 163840 | tf_op jit(solution)/shard_map/psum | solution.py:29
  8.3 82.1 %copy-start = (bf16[512,512]{1,0:T(8,128)(2,1)S(1)}, bf16[512,512]{1,0:T(8,128)(2,1)}, u32[]{:S(2)}) copy-start(bf16[512,512]{1,0:T(8,128)(2,1)} %param.3) | copy-start | bytes 1572868
  10.4 169.3 %reduce-scatter.5.cloned.1.call-start = ((), (), s32[]{:S(2)}) async-start(), calls=%async_computation.5 | async-start | bytes 589824 | tf_op jit(solution)/shard_map/reduce_scatter | solution.py:47
  82.5 0.9 copy-start.4
  82.5 7.4 %copy-start.5 = (f32[31,512]{1,0:T(8,128)S(1)}, f32[31,512]{1,0:T(8,128)}, u32[]{:S(2)}) copy-start(f32[31,512]{1,0:T(8,128)} %get-tuple-element.5) | copy-start | bytes 190468
  111.9 6.8 %collective-permute-start = (bf16[512,512]{1,0:T(8,128)(2,1)S(1)}, bf16[512,512]{1,0:T(8,128)(2,1)S(1)}, u32[]{:S(2)}, u32[]{:S(2)}) collective-permute-start(bf16[512,512]{1,0:T(8,128)(2,1)S(1)} %multiply_convert_fusion), channel_id=1, source_target_pairs={{1,0},{2,1},{3,2},{0,3},{5,4},{6,5},{7,6},{4,7},{9,8},{10,9},{11,1... | collective-permute-start | bytes 1572872 | tf_op jit(solution)/shard_map/ppermute | solution.py:14
  119.9 124.4 %reduce-scatter.3.cloned.1.call-start = ((), (), s32[]{:S(2)}) async-start(), calls=%async_computation.4 | async-start | bytes 589824 | tf_op jit(solution)/shard_map/reduce_scatter | solution.py:47
  120.0 8.7 %collective-permute-start.1 = (bf16[512,512]{1,0:T(8,128)(2,1)S(1)}, bf16[512,512]{1,0:T(8,128)(2,1)S(1)}, u32[]{:S(2)}, u32[]{:S(2)}) collective-permute-start(bf16[512,512]{1,0:T(8,128)(2,1)S(1)} %collective-permute-done), channel_id=1, source_target_pairs={{1,0},{2,1},{3,2},{0,3},{5,4},{6,5},{7,6},{4,7},{9,8},{10,9},{11,1... | collective-permute-start | bytes 1572872 | tf_op jit(solution)/shard_map/ppermute | solution.py:14
  181.5 10.5 %all-to-all-start.1 = ((bf16[8,2,2048]{2,1,0:T(2,128)(2,1)}), bf16[8,2,2048]{2,1,0:T(2,128)(2,1)S(1)}, u32[]{:S(2)}, u32[]{:S(2)}) async-start(bf16[8,2,2048]{2,1,0:T(2,128)(2,1)} %reshape.24), calls=%async_computation.3 | async-start | bytes 131072 | tf_op jit(solution)/shard_map/all_to_all | solution.py:51
  185.1 0.7 copy-start.6
  192.1 0.8 copy-start.3
  192.2 57.5 %collective-permute-start.3 = (bf16[512,64]{0,1:T(8,128)(2,1)S(1)}, bf16[512,64]{0,1:T(8,128)(2,1)S(1)}, u32[]{:S(2)}, u32[]{:S(2)}) collective-permute-start(bf16[512,64]{0,1:T(8,128)(2,1)S(1)} %copy.16), channel_id=1, source_target_pairs={{3,0},{0,1},{1,2},{2,3},{7,4},{4,5},{5,6},{6,7},{11,8},{8,9},{9,10... | collective-permute-start | bytes 196616 | tf_op jit(solution)/shard_map/ppermute | solution.py:14
  246.1 10.6 %all-to-all-start = ((bf16[8,2,2048]{2,1,0:T(2,128)(2,1)}), bf16[8,2,2048]{2,1,0:T(2,128)(2,1)S(1)}, u32[]{:S(2)}, u32[]{:S(2)}) async-start(bf16[8,2,2048]{2,1,0:T(2,128)(2,1)} %reshape.26), calls=%async_computation.1 | async-start | bytes 131072 | tf_op jit(solution)/shard_map/all_to_all | solution.py:51
  256.9 1.7 copy-start.2
  257.1 4.3 %collective-permute-start.2 = (bf16[512,64]{0,1:T(8,128)(2,1)S(1)}, bf16[512,64]{0,1:T(8,128)(2,1)S(1)}, u32[]{:S(2)}, u32[]{:S(2)}) collective-permute-start(bf16[512,64]{0,1:T(8,128)(2,1)S(1)} %all_to_all.31), channel_id=1, source_target_pairs={{2,0},{3,1},{0,2},{1,3},{6,4},{7,5},{4,6},{5,7},{10,8},{11,9},{8,1... | collective-permute-start | bytes 196616 | tf_op jit(solution)/shard_map/ppermute | solution.py:14
Sparse Core Ops, SparseCore 0:
  10.8 71.6 all-reduce.3
  120.0 59.6 reduce-scatter.4
  183.4 60.8 reduce-scatter.2
where the time goes:
time: 269 us
  waiting for transfers between devices  201 us (75%)
  blocking collectives  20.2 us (8%)
  between operations  14.5 us (5%)
  starting transfers between devices  10.9 us (4%)
  matrix products  7.97 us (3%)
  other arithmetic  7.43 us (3%)
  local copies, waits for them, and re-layouts  7 us (3%)
    reduce_scatter x2, waiting for transfers between devices, shards(): lax.psum_scatter(partial_tile.astype(jnp.bfloat16), 'sample', scatter_dim...  101 us
    psum x1, waiting for transfers between devices, shards(): moment, cross = lax.psum((moment_local, cross_local), 'sample')  72 us
    psum x1, blocking collectives, shards(): spread = lax.psum(jnp.sum(residual * residual, 0), 'sample')  20.2 us
    ppermute x4, waiting for transfers between devices, passed_along(): return lax.ppermute(block, axis, route)  16.2 us
    all_to_all x2, waiting for transfers between devices, shards(): lax.all_to_all(finished, 'sample', split_axis=1, concat_axis=0, tiled=True)  11.2 us
    all_to_all x2, starting transfers between devices, shards(): lax.all_to_all(finished, 'sample', split_axis=1, concat_axis=0, tiled=True)  7.25 us
  transfers between devices with their start and end apart: 9, of which 8 were waited for; matrix products, arithmetic and copies ran while one was open for 2% of the time, Pallas kernels for 0%

commit v1 on v0

v1 whole, which is shorter than its diff:
```python
import functools
import math

import jax
import jax.numpy as jnp
from jax import lax
from jax.experimental import pallas as pl
from jax.experimental.pallas import tpu as pltpu
from jax.sharding import PartitionSpec as P

MAXR = 2
ROWS = 8
LANES = 128
MESH = pl.DeviceIdType.MESH
HIGHEST = lax.Precision.HIGHEST
F32 = jnp.float32
BF16 = jnp.bfloat16


def exact_dot(a, b, dims):
    return lax.dot_general(a, b, (dims, ((), ())), precision=HIGHEST, preferred_element_type=F32)


def fast_dot(a, b, dims):
    return lax.dot_general(a, b, (dims, ((), ())), preferred_element_type=F32)


def inverse(matrix):
    size = matrix.shape[0]
    row_at = lax.broadcasted_iota(jnp.int32, matrix.shape, 0)
    lane_at = lax.broadcasted_iota(jnp.int32, matrix.shape, 1)

    def step(k, a):
        row = jnp.sum(jnp.where(row_at == k, a, 0.0), 0, keepdims=True)
        column = jnp.sum(jnp.where(lane_at == k, a, 0.0), 1, keepdims=True)
        pivot = jnp.sum(jnp.where(lane_at[:1] == k, row, 0.0), 1, keepdims=True)
        row = jnp.where(lane_at[:1] == k, 1.0, row) / pivot
        rest = jnp.where(lane_at == k, 0.0, a) - column * row
        return jnp.where(row_at == k, row, rest)

    return lax.fori_loop(0, size, step, matrix)


def kernel(
    ns, nb, dosage, covariates, out,
    design, cross, cross_out, cross_in, cross_sum, moments, coefs, blocks, own_t, others,
    spreads, tiles, pair_out, pair_in, ring_out, ring_in, turn_out, turn_in, back_out, back_in,
    block_send, block_recv, cross_send, cross_recv, moment_send, moment_recv, sum_send, sum_recv,
    coef_send, coef_recv, spread_send, spread_recv, pair_send, pair_recv, ring_send, ring_recv,
    turn_send, turn_recv, back_send, back_recv,
):
    s = lax.axis_index("sample")
    v = lax.axis_index("variant")
    local, width = dosage.shape
    terms = covariates.shape[0] + 1
    depth = cross.shape[0]
    across = ns // (depth // ROWS)
    piece = width // across
    groups = ns // 2
    group, half = lax.div(s, 2), lax.rem(s, 2)
    rows = width // ns

    def sample_peer(j):
        return lax.rem(s + j, ns)

    def variant_peer(j):
        return lax.rem(v + j + nb, nb)

    def copy(src, dst, send, recv, sample, variant):
        return pltpu.make_async_remote_copy(
            src_ref=src, dst_ref=dst, send_sem=send, recv_sem=recv,
            device_id=(sample, variant), device_id_type=MESH,
        )

    barrier = pltpu.get_barrier_semaphore()
    hops = sorted({1, 2, nb - 1, nb - 2})
    for j in range(1, ns):
        pl.semaphore_signal(barrier, inc=1, device_id=(sample_peer(j), v), device_id_type=MESH)
    for j in hops:
        pl.semaphore_signal(barrier, inc=1, device_id=(s, variant_peer(j)), device_id_type=MESH)

    design[...] = jnp.zeros_like(design)
    design[0:1] = jnp.ones((1, local), F32)
    design[1:terms] = covariates[...]
    full = design[0:depth]
    high = full.astype(BF16)
    left = full - high.astype(F32)
    middle = left.astype(BF16)
    low = (left - middle.astype(F32)).astype(BF16)
    genotype = dosage[...]
    contract = ((1,), (0,))
    partial = fast_dot(high, genotype, contract) + (
        fast_dot(middle, genotype, contract) + fast_dot(low, genotype, contract)
    )
    for i in range(ns):
        r, c = divmod(i, across)
        cross_out[i] = partial[r * ROWS : (r + 1) * ROWS, c * piece : (c + 1) * piece]
    moments[s] = exact_dot(full, design[...], ((1,), (1,)))

    pl.semaphore_wait(barrier, ns - 1 + len(hops))

    sent = []

    def start(c):
        c.start()
        sent.append(c)

    for j in range(1, ns):
        p = sample_peer(j)
        start(copy(cross_out.at[p], cross_in.at[s], cross_send.at[j], cross_recv.at[j], p, v))
    for j in range(1, ns):
        p = sample_peer(j)
        start(copy(moments.at[s], moments.at[s], moment_send.at[j], moment_recv.at[j], p, v))
    behind = variant_peer(-1)
    start(copy(dosage, blocks.at[0], block_send.at[0], block_recv.at[0], s, behind))

    own_t[...] = genotype.astype(F32).T

    total = cross_out[s]
    for j in range(1, ns):
        q = sample_peer(ns - j)
        copy(cross_out.at[q], cross_in.at[q], cross_send.at[j], cross_recv.at[j], q, v).wait_recv()
        total = total + cross_in[q]
    cross_sum[s] = total
    for j in range(1, ns):
        p = sample_peer(j)
        start(copy(cross_sum.at[s], cross_sum.at[s], sum_send.at[j], sum_recv.at[j], p, v))

    moment = moments[s]
    for j in range(1, ns):
        q = sample_peer(ns - j)
        copy(moments.at[q], moments.at[q], moment_send.at[j], moment_recv.at[j], q, v).wait_recv()
        moment = moment + moments[q]
    row_at = lax.broadcasted_iota(jnp.int32, moment.shape, 0)
    lane_at = lax.broadcasted_iota(jnp.int32, moment.shape, 1)
    moment = jnp.where((row_at == lane_at) & (row_at >= terms), 1.0, moment)
    solve = inverse(moment)[:, :depth]

    for j in range(1, ns):
        q = sample_peer(ns - j)
        copy(cross_sum.at[q], cross_sum.at[q], sum_send.at[j], sum_recv.at[j], q, v).wait_recv()
    for i in range(ns):
        r, c = divmod(i, across)
        cross[r * ROWS : (r + 1) * ROWS, c * piece : (c + 1) * piece] = cross_sum[i]
    coefs[0] = exact_dot(solve, cross[...], contract)
    for k in (1, 2):
        start(copy(coefs.at[0], coefs.at[k], coef_send.at[k], coef_recv.at[k], s, variant_peer(-k)))
    copy(dosage, blocks.at[0], block_send.at[0], block_recv.at[0], s, behind).wait_recv()
    start(copy(blocks.at[0], blocks.at[1], block_send.at[1], block_recv.at[1], s, behind))

    ones = jnp.ones((ROWS, local), F32)
    mine = own_t[...] - exact_dot(coefs[0], full, ((0,), (0,)))
    own_t[...] = mine
    spreads[s, 0:1] = exact_dot(ones, mine * mine, ((1,), (1,)))[0:1]
    for k in (1, 2):
        copy(coefs.at[0], coefs.at[k], coef_send.at[k], coef_recv.at[k], s, behind).wait_recv()
        if k == 2:
            copy(blocks.at[0], blocks.at[1], block_send.at[1], block_recv.at[1], s, behind).wait_recv()
        theirs = blocks[k - 1].astype(F32) - exact_dot(full, coefs[k], ((0,), (0,)))
        spreads[s, k : k + 1] = jnp.sum(theirs * theirs, 0, keepdims=True)
        others[:, (k - 1) * width : k * width] = theirs.astype(BF16)
    spreads[s, 3:ROWS] = jnp.zeros((ROWS - 3, width), F32)
    partner = group * 2 + 1 - half
    order = list(range(1, groups)) + [0]
    for j in order:
        g = lax.rem(group + j, groups)
        lhs = own_t[pl.ds(pl.multiple_of(g * 2 * rows, 2 * rows), 2 * rows)].astype(BF16)
        tiles[j] = fast_dot(lhs, others[...], contract)
        pair_out[j] = tiles[j, pl.ds(pl.multiple_of((1 - half) * rows, rows), rows)].astype(BF16)
        start(copy(pair_out.at[j], pair_in.at[j], pair_send.at[j], pair_recv.at[j], partner, v))
    for j in range(1, ns):
        p = sample_peer(j)
        start(copy(spreads.at[s], spreads.at[s], spread_send.at[j], spread_recv.at[j], p, v))
    for j in order:
        copy(pair_out.at[j], pair_in.at[j], pair_send.at[j], pair_recv.at[j], partner, v).wait_recv()
        mine = tiles[j, pl.ds(pl.multiple_of(half * rows, rows), rows)]
        summed = mine + pair_in[j].astype(F32)
        if j:
            ring_out[j] = summed.astype(BF16)
            target = lax.rem(group + j, groups) * 2 + half
            start(copy(ring_out.at[j], ring_in.at[j], ring_send.at[j], ring_recv.at[j], target, v))

    spread = spreads[s]
    for j in range(1, ns):
        q = sample_peer(ns - j)
        copy(spreads.at[q], spreads.at[q], spread_send.at[j], spread_recv.at[j], q, v).wait_recv()
        spread = spread + spreads[q]
    samples = float(local * ns)
    scale = jnp.sqrt(samples / spread[0:3])
    chosen = lax.broadcasted_iota(jnp.int32, (rows, width), 1) == (
        lax.broadcasted_iota(jnp.int32, (rows, width), 0) + s * rows
    )
    scale_rows = jnp.sum(jnp.where(chosen, scale[0:1], 0.0), 1, keepdims=True)
    scale_rows = scale_rows * (1.0 / math.sqrt(samples))

    for j in range(1, groups):
        copy(ring_out.at[j], ring_in.at[j], ring_send.at[j], ring_recv.at[j], partner, v).wait_recv()
        summed = summed + ring_in[j].astype(F32)
    finished = []
    for k in (1, 2):
        part = summed[:, (k - 1) * width : k * width] * scale_rows * scale[k : k + 1]
        out[MAXR + k - 1] = part.astype(BF16)
        finished.append(part)

    for i in range(ns):
        turn_out[i] = jnp.concatenate(
            [part[:, i * rows : (i + 1) * rows] for part in finished], 1
        ).astype(BF16)
    for j in range(1, ns):
        p = sample_peer(j)
        start(copy(turn_out.at[p], turn_in.at[s], turn_send.at[j], turn_recv.at[j], p, v))
    turn_in[s] = turn_out[s]
    for j in range(1, ns):
        q = sample_peer(ns - j)
        copy(turn_out.at[q], turn_in.at[q], turn_send.at[j], turn_recv.at[j], q, v).wait_recv()
    turned = turn_in[...].astype(F32).reshape(width, 2 * rows).T.astype(BF16)
    ends = [k for k in (1, 2) if 2 * k % nb]
    for k in ends:
        back_out[k - 1] = turned[(k - 1) * rows : k * rows]
        start(copy(back_out.at[k - 1], back_in.at[k - 1], back_send.at[k - 1], back_recv.at[k - 1],
                   s, variant_peer(k)))
    for k in (1, 2):
        if k in ends:
            copy(back_out.at[k - 1], back_in.at[k - 1], back_send.at[k - 1], back_recv.at[k - 1],
                 s, behind).wait_recv()
            out[MAXR - k] = back_in[k - 1]
        else:
            out[MAXR - k] = finished[k - 1].astype(BF16)
    for c in sent:
        c.wait_send()


def shards(dosage, covariates, reach):
    ns, nb = lax.axis_size("sample"), lax.axis_size("variant")
    local, width = dosage.shape
    depth = -(-(covariates.shape[0] + 1) // 32) * 32
    piece = width * (depth // ROWS) // ns
    groups, rows = ns // 2, width // ns
    vmem = lambda shape, dtype: pltpu.VMEM(shape, dtype)
    pair = lambda n: [pltpu.SemaphoreType.DMA((n,))] * 2
    found = pl.pallas_call(
        functools.partial(kernel, ns, nb),
        out_shape=jax.ShapeDtypeStruct((2 * MAXR, rows, width), BF16),
        in_specs=[pl.BlockSpec(memory_space=pltpu.VMEM)] * 2,
        out_specs=pl.BlockSpec(memory_space=pltpu.VMEM),
        scratch_shapes=[
            vmem((LANES, local), F32),
            vmem((depth, width), F32),
            vmem((ns, ROWS, piece), F32),
            vmem((ns, ROWS, piece), F32),
            vmem((ns, ROWS, piece), F32),
            vmem((ns, depth, LANES), F32),
            vmem((3, depth, width), F32),
            vmem((2, local, width), BF16),
            vmem((width, local), F32),
            vmem((local, 2 * width), BF16),
            vmem((ns, ROWS, width), F32),
            vmem((groups, 2 * rows, 2 * width), F32),
            vmem((groups, rows, 2 * width), BF16),
            vmem((groups, rows, 2 * width), BF16),
            vmem((groups, rows, 2 * width), BF16),
            vmem((groups, rows, 2 * width), BF16),
            vmem((ns, rows, 2 * rows), BF16),
            vmem((ns, rows, 2 * rows), BF16),
            vmem((2, rows, width), BF16),
            vmem((2, rows, width), BF16),
            *pair(2), *pair(ns), *pair(ns), *pair(ns), *pair(3), *pair(ns), *pair(groups),
            *pair(groups), *pair(ns), *pair(2),
        ],
        compiler_params=pltpu.CompilerParams(
            collective_id=0, has_side_effects=True, vmem_limit_bytes=40 * 1024 * 1024
        ),
    )(dosage, covariates)
    distance = jnp.array([abs(m - MAXR if m < MAXR else m - MAXR + 1) for m in range(2 * MAXR)])
    live = distance <= reach[lax.axis_index("variant")]
    return jnp.where(live[:, None, None], found, jnp.zeros_like(found))


def solution(mesh):
    placed = (P("sample", "variant"), P(None, "sample"), P())
    return jax.shard_map(
        shards,
        mesh=mesh,
        in_specs=placed,
        out_specs=P(None, ("variant", "sample"), None),
        check_vma=False,
    )
```

time: 269 us -> 53.3 us (0.20)
  waiting for transfers between devices: 201 us -> 0 us
  Pallas kernels: 0 us -> 47.9 us
  blocking collectives: 20.2 us -> 0 us
  between operations: 14.5 us -> 0.03 us
  starting transfers between devices: 10.9 us -> 0 us
  matrix products: 7.97 us -> 0 us
  other arithmetic: 7.43 us -> 1.44 us
  local copies, waits for them, and re-layouts: 7 us -> 3.77 us
    reduce_scatter x2 -> x0, waiting for transfers between devices: 101 us -> none  [shards(): lax.psum_scatter(partial_tile.astype(jnp.bfloat16), 'sample', scatter_dim...]
    psum x1 -> x0, waiting for transfers between devices: 72 us -> none  [shards(): moment, cross = lax.psum((moment_local, cross_local), 'sample')]
    pallas_call x0 -> x1, Pallas kernels: none -> 47.9 us  [shards(): pl.pallas_call(functools.partial(kernel, ns, nb), out_shape=jax.ShapeDtyp...]
    psum x1 -> x0, blocking collectives: 20.2 us -> none  [shards(): spread = lax.psum(jnp.sum(residual * residual, 0), 'sample')]
    ppermute x4 -> x0, waiting for transfers between devices: 16.2 us -> none  [passed_along(): return lax.ppermute(block, axis, route)]
    all_to_all x2 -> x0, waiting for transfers between devices: 11.2 us -> none  [shards(): lax.all_to_all(finished, 'sample', split_axis=1, concat_axis=0, tiled=True)]
    dot_general x5 -> x0, matrix products: 7.5 us -> none  [the longest x2 2.52 us: shards(): lax.dot_general(scaled, ahead, (((0,), (0,)), ((), ())), preferred_elemen...]
    another operation x10 -> x0, other arithmetic: 7.29 us -> none  [the longest x3 3.5 us: shards(): factor = jnp.linalg.cholesky(moment)]
  transfers between devices with their start and end apart: 9 -> 0, of which waited for: 8 -> 0; matrix products, arithmetic and copies ran while one was open for 2% -> 0% of each run, Pallas kernels for 0% -> 0%
where the time goes in v1:
time: 53.3 us; the launch traced here: 53.1 us
  Pallas kernels  47.9 us (90%)
  local copies, waits for them, and re-layouts  3.77 us (7%)
  other arithmetic  1.44 us (3%)
    pallas_call x1, Pallas kernels, shards(): pl.pallas_call(functools.partial(kernel, ns, nb), out_shape=jax.ShapeDtyp...  47.9 us
    unnamed x8, local copies, waits for them, and re-layouts  3.19 us

profile of v1, /device:TPU:0, one launch (start us, length us, event | category | flops | bytes accessed | tf_op | source)
XLA Modules:
  0.0 53.1 jit_solution(16824195577944008387)
XLA Ops:
  0.0 0.0 copy-start.2
  0.0 0.7 %copy-done.2 = s32[4]{0:T(128)S(1)} copy-done((s32[4]{0:T(128)S(1)}, s32[4]{0:T(128)}, u32[]{:S(2)}) %copy-start.2) | copy-done | bytes 40
  0.7 0.6 %dynamic_slice.3 = s32[1]{0:T(128)} dynamic-slice(s32[4]{0:T(128)S(1)} %copy-done.2, s32[]{:T(128)S(6)} %select_n.7), dynamic_slice_sizes={1} | dynamic-slice | bytes 12 | tf_op jit(solution)/shard_map/dynamic_slice | solution.py:275
  1.2 0.0 copy-start.3
  1.2 0.7 %copy-done.3 = s32[4]{0:T(128)S(1)} copy-done((s32[4]{0:T(128)S(1)}, s32[4]{0:T(128)}, u32[]{:S(2)}) %copy-start.3) | copy-done | bytes 40
  1.9 0.6 %broadcast_compare_fusion = pred[4]{0:T(512)(128)(4,1)S(1)} fusion(s32[4]{0:T(128)S(1)} %copy-done.3, s32[]{:T(128)} %bitcast), kind=kLoop, calls=%fused_computation.1 | loop fusion | flops 4 | bytes 24 | tf_op jit(solution)/shard_map/le | solution.py:275
  2.6 0.0 copy-start
  2.6 1.0 %copy-done = bf16[512,512]{1,0:T(8,128)(2,1)S(1)} copy-done((bf16[512,512]{1,0:T(8,128)(2,1)S(1)}, bf16[512,512]{1,0:T(8,128)(2,1)}, u32[]{:S(2)}) %copy-start) | copy-done | bytes 524312
  3.6 0.0 copy-start.1
  3.6 0.8 %copy-done.1 = f32[30,512]{1,0:T(8,128)S(1)} copy-done((f32[30,512]{1,0:T(8,128)S(1)}, f32[30,512]{1,0:T(8,128)}, u32[]{:S(2)}) %copy-start.1) | copy-done | bytes 61464
  4.4 47.9 %shard_map.46 = bf16[4,64,512]{2,1,0:T(8,128)(2,1)S(1)} custom-call(bf16[512,512]{1,0:T(8,128)(2,1)S(1)} %copy-done, f32[30,512]{1,0:T(8,128)S(1)} %copy-done.1), custom_call_target="tpu_custom_call" | custom-call | tf_op jit(solution)/shard_map/pallas_call | solution.py:241
  52.3 0.8 %broadcast_select_fusion = bf16[4,64,512]{2,1,0:T(8,128)(2,1)} fusion(bf16[4,64,512]{2,1,0:T(8,128)(2,1)S(1)} %shard_map.46, pred[4]{0:T(512)(128)(4,1)S(1)} %broadcast_compare_fusion), kind=kLoop, calls=%fused_computation | loop fusion | flops 131072 | bytes 524292 | tf_op jit(solution)/shard_map/jit(_where)/select_n | solution.py:276
Async XLA Ops:
  0.0 0.7 %copy-start.2 = (s32[4]{0:T(128)S(1)}, s32[4]{0:T(128)}, u32[]{:S(2)}) copy-start(s32[4]{0:T(128)} %param.6) | copy-start | bytes 52
  1.2 0.7 %copy-start.3 = (s32[4]{0:T(128)S(1)}, s32[4]{0:T(128)}, u32[]{:S(2)}) copy-start(s32[4]{0:T(128)} %constant.12.clone) | copy-start | bytes 52
  2.6 1.0 %copy-start = (bf16[512,512]{1,0:T(8,128)(2,1)S(1)}, bf16[512,512]{1,0:T(8,128)(2,1)}, u32[]{:S(2)}) copy-start(bf16[512,512]{1,0:T(8,128)(2,1)} %dosage.1) | copy-start | bytes 1572868
  3.6 0.8 %copy-start.1 = (f32[30,512]{1,0:T(8,128)S(1)}, f32[30,512]{1,0:T(8,128)}, u32[]{:S(2)}) copy-start(f32[30,512]{1,0:T(8,128)} %covariates.1) | copy-start | bytes 184324

commit v2 on v1

v2 whole, which is shorter than its diff:
```python
import functools
import math

import jax
import jax.numpy as jnp
from jax import lax
from jax.experimental import pallas as pl
from jax.experimental.pallas import tpu as pltpu
from jax.sharding import PartitionSpec as P

MAXR = 2
ROWS = 8
LANES = 128
MESH = pl.DeviceIdType.MESH
HIGHEST = lax.Precision.HIGHEST
F32 = jnp.float32
BF16 = jnp.bfloat16


def exact_dot(a, b, dims):
    return lax.dot_general(a, b, (dims, ((), ())), precision=HIGHEST, preferred_element_type=F32)


def pieces(x):
    high = x.astype(BF16)
    left = x - high.astype(F32)
    middle = left.astype(BF16)
    return high, middle, (left - middle.astype(F32)).astype(BF16)


def left_terms(x, axis):
    h, m, l = pieces(x)
    return jnp.concatenate([h, h, m, h, m, l], axis)


def right_terms(x, axis):
    h, m, l = pieces(x)
    return jnp.concatenate([h, m, h, l, m, h], axis)


def fast_dot(a, b, dims):
    return lax.dot_general(a, b, (dims, ((), ())), preferred_element_type=F32)


def eliminate(matrix, first, last):
    row_at = lax.broadcasted_iota(jnp.int32, matrix.shape, 0)
    lane_at = lax.broadcasted_iota(jnp.int32, matrix.shape, 1)

    def step(k, a):
        row = jnp.sum(jnp.where(row_at == k, a, 0.0), 0, keepdims=True)
        column = jnp.sum(jnp.where(lane_at == k, a, 0.0), 1, keepdims=True)
        pivot = jnp.sum(jnp.where(lane_at[:1] == k, row, 0.0), 1, keepdims=True)
        row = jnp.where(lane_at[:1] == k, 1.0, row) / pivot
        rest = jnp.where(lane_at == k, 0.0, a) - column * row
        return jnp.where(row_at == k, row, rest)

    return lax.fori_loop(first, last, step, matrix)


def kernel(
    ns, nb, dosage_in, covariates_in, reach_in, out,
    dosage, covariates, reach, design, terms_ref, cross, cross_out, cross_in, cross_sum, moments,
    coefs, blocks, own_t, own_b, others, spreads, tiles, pair_out, pair_in, ring_out, ring_in,
    turn_out, turn_in, back_out, back_in, load_sem,
    block_send, block_recv, cross_send, cross_recv, moment_send, moment_recv, sum_send, sum_recv,
    coef_send, coef_recv, spread_send, spread_recv, pair_send, pair_recv, ring_send, ring_recv,
    turn_send, turn_recv, back_send, back_recv,
):
    s = lax.axis_index("sample")
    v = lax.axis_index("variant")
    local, width = dosage.shape
    terms = covariates.shape[0] + 1
    depth = cross.shape[0]
    across = ns // (depth // ROWS)
    piece = width // across
    groups = ns // 2
    group, half = lax.div(s, 2), lax.rem(s, 2)
    rows = width // ns
    samples = float(local * ns)

    def sample_peer(j):
        return lax.rem(s + j, ns)

    def variant_peer(j):
        return lax.rem(v + j + nb, nb)

    def copy(src, dst, send, recv, sample, variant):
        return pltpu.make_async_remote_copy(
            src_ref=src, dst_ref=dst, send_sem=send, recv_sem=recv,
            device_id=(sample, variant), device_id_type=MESH,
        )

    load_dosage = pltpu.make_async_copy(dosage_in, dosage, load_sem.at[0])
    load_covariates = pltpu.make_async_copy(covariates_in, covariates, load_sem.at[1])
    load_reach = pltpu.make_async_copy(reach_in, reach, load_sem.at[2])
    load_covariates.start()
    load_dosage.start()
    load_reach.start()

    barrier = pltpu.get_barrier_semaphore()
    hops = sorted({1, 2, nb - 1, nb - 2})
    for j in range(1, ns):
        pl.semaphore_signal(barrier, inc=1, device_id=(sample_peer(j), v), device_id_type=MESH)
    for j in hops:
        pl.semaphore_signal(barrier, inc=1, device_id=(s, variant_peer(j)), device_id_type=MESH)

    sent = []

    def start(c):
        c.start()
        sent.append(c)

    contract = ((1,), (0,))
    design[...] = jnp.zeros_like(design)
    design[0:1] = jnp.ones((1, local), F32)
    load_covariates.wait()
    design[1:terms] = covariates[...]
    full = design[0:depth]
    high, middle, low = pieces(full)
    moments[s] = exact_dot(full, design[...], ((1,), (1,)))
    load_dosage.wait()
    genotype = dosage[...]
    partial = fast_dot(jnp.concatenate([high, middle, low], 0), genotype, contract)
    partial = partial[:depth] + (partial[depth : 2 * depth] + partial[2 * depth :])
    for i in range(ns):
        r, c = divmod(i, across)
        cross_out[i] = partial[r * ROWS : (r + 1) * ROWS, c * piece : (c + 1) * piece]

    pl.semaphore_wait(barrier, ns - 1 + len(hops))
    for j in range(1, ns):
        p = sample_peer(j)
        start(copy(moments.at[s], moments.at[s], moment_send.at[j], moment_recv.at[j], p, v))
        start(copy(cross_out.at[p], cross_in.at[s], cross_send.at[j], cross_recv.at[j], p, v))
    behind = variant_peer(-1)
    start(copy(dosage, blocks.at[0], block_send.at[0], block_recv.at[0], s, behind))

    terms_ref[...] = left_terms(full, 0)
    own_t[...] = genotype.astype(F32).T

    moment = moments[s]
    for j in range(1, ns):
        q = sample_peer(ns - j)
        copy(moments.at[q], moments.at[q], moment_send.at[j], moment_recv.at[j], q, v).wait_recv()
        moment = moment + moments[q]
    row_at = lax.broadcasted_iota(jnp.int32, moment.shape, 0)
    lane_at = lax.broadcasted_iota(jnp.int32, moment.shape, 1)
    moment = jnp.where((row_at == lane_at) & (row_at >= terms), 1.0, moment)
    solve = eliminate(moment, 0, depth // 4)

    total = cross_out[s]
    for j in range(1, ns):
        q = sample_peer(ns - j)
        copy(cross_out.at[q], cross_in.at[q], cross_send.at[j], cross_recv.at[j], q, v).wait_recv()
        total = total + cross_in[q]
    cross_sum[s] = total
    for j in range(1, ns):
        p = sample_peer(j)
        start(copy(cross_sum.at[s], cross_sum.at[s], sum_send.at[j], sum_recv.at[j], p, v))
    solve = eliminate(solve, depth // 4, depth)[:, :depth]

    for j in range(1, ns):
        q = sample_peer(ns - j)
        copy(cross_sum.at[q], cross_sum.at[q], sum_send.at[j], sum_recv.at[j], q, v).wait_recv()
    for i in range(ns):
        r, c = divmod(i, across)
        cross[r * ROWS : (r + 1) * ROWS, c * piece : (c + 1) * piece] = cross_sum[i]
    coefs[0] = exact_dot(solve, cross[...], contract)
    for k in (1, 2):
        start(copy(coefs.at[0], coefs.at[k], coef_send.at[k], coef_recv.at[k], s, variant_peer(-k)))
    copy(dosage, blocks.at[0], block_send.at[0], block_recv.at[0], s, behind).wait_recv()
    start(copy(blocks.at[0], blocks.at[1], block_send.at[1], block_recv.at[1], s, behind))

    mine = own_t[...] - fast_dot(right_terms(coefs[0], 0), terms_ref[...], ((0,), (0,)))
    own_b[...] = mine.astype(BF16)
    own_t[...] = mine
    partner = group * 2 + 1 - half
    order = list(range(1, groups)) + [0]

    def residual(k):
        copy(coefs.at[0], coefs.at[k], coef_send.at[k], coef_recv.at[k], s, behind).wait_recv()
        if k == 2:
            copy(blocks.at[0], blocks.at[1], block_send.at[1], block_recv.at[1], s, behind).wait_recv()
        fitted = fast_dot(terms_ref[...], right_terms(coefs[k], 0), ((0,), (0,)))
        theirs = blocks[k - 1].astype(F32) - fitted
        others[...] = theirs.astype(BF16)
        spreads[s, k : k + 1] = jnp.sum(theirs * theirs, 0, keepdims=True)

    def slot(k, j):
        return (k - 1) * groups + j

    def pair_copy(k, j):
        i = slot(k, j)
        return copy(pair_out.at[i], pair_in.at[i], pair_send.at[i], pair_recv.at[i], partner, v)

    def ring_copy(k, j):
        i = slot(k, j)
        target = lax.rem(group + j, groups) * 2 + half
        return copy(ring_out.at[i], ring_in.at[i], ring_send.at[i], ring_recv.at[i], target, v)

    def give(k, j):
        i = slot(k, j)
        g = lax.rem(group + j, groups)
        lhs = own_b[pl.ds(pl.multiple_of(g * 2 * rows, 2 * rows), 2 * rows)]
        tiles[i] = fast_dot(lhs, others[...], contract)
        pair_out[i] = tiles[i, pl.ds(pl.multiple_of((1 - half) * rows, rows), rows)].astype(BF16)
        start(pair_copy(k, j))

    def take(k, j):
        i = slot(k, j)
        pair_copy(k, j).wait_recv()
        summed = tiles[i, pl.ds(pl.multiple_of(half * rows, rows), rows)] + pair_in[i].astype(F32)
        if j:
            ring_out[i] = summed.astype(BF16)
            start(ring_copy(k, j))
        return summed

    def gather(k, summed):
        for j in range(1, groups):
            ring_copy(k, j).wait_recv()
            summed = summed + ring_in[slot(k, j)].astype(F32)
        return summed

    residual(1)
    for j in order:
        give(1, j)
    column = jnp.sum(mine * mine, 1, keepdims=True)
    spreads[s, 0:1] = jnp.broadcast_to(column, (width, LANES)).T[0:1]
    spreads[s, 3:ROWS] = jnp.zeros((ROWS - 3, width), F32)
    for j in order[:1]:
        take(1, j)
    residual(2)
    for j in range(1, ns):
        p = sample_peer(j)
        start(copy(spreads.at[s], spreads.at[s], spread_send.at[j], spread_recv.at[j], p, v))
    for n, j in enumerate(order):
        give(2, j)
        if n:
            last = take(1, j)

    spread = spreads[s]
    for j in range(1, ns):
        q = sample_peer(ns - j)
        copy(spreads.at[q], spreads.at[q], spread_send.at[j], spread_recv.at[j], q, v).wait_recv()
        spread = spread + spreads[q]
    scale = jnp.sqrt(samples / spread[0:3])
    chosen = lax.broadcasted_iota(jnp.int32, (rows, width), 1) == (
        lax.broadcasted_iota(jnp.int32, (rows, width), 0) + s * rows
    )
    scale_rows = jnp.sum(jnp.where(chosen, scale[0:1], 0.0), 1, keepdims=True)
    scale_rows = scale_rows * (1.0 / math.sqrt(samples))
    load_reach.wait()
    own_reach = reach[v]

    def masked(k, tile):
        return jnp.where(own_reach >= k, tile.astype(F32), 0.0).astype(BF16)

    def finish(k, summed):
        part = summed * scale_rows * scale[k : k + 1]
        out[MAXR + k - 1] = masked(k, part)
        return part

    def turn_copy(k, j, p, q):
        return copy(turn_out.at[k - 1, p], turn_in.at[k - 1, q], turn_send.at[(k - 1) * ns + j],
                    turn_recv.at[(k - 1) * ns + j], p, v)

    def turn_start(k, part):
        for i in range(ns):
            turn_out[k - 1, i] = part[:, i * rows : (i + 1) * rows].astype(BF16)
        for j in range(1, ns):
            start(turn_copy(k, j, sample_peer(j), s))
        turn_in[k - 1, s] = turn_out[k - 1, s]

    def back_copy(k):
        return copy(back_out.at[k - 1], back_in.at[k - 1], back_send.at[k - 1],
                    back_recv.at[k - 1], s, variant_peer(k))

    def turn_end(k):
        for j in range(1, ns):
            q = sample_peer(ns - j)
            turn_copy(k, j, q, q).wait_recv()
        back_out[k - 1] = turn_in[k - 1].astype(F32).reshape(width, rows).T.astype(BF16)
        start(back_copy(k))

    def back_end(k):
        back_copy(k).wait_recv()
        out[MAXR - k] = masked(k, back_in[k - 1])

    early = len(order) // 2
    for j in order[:early]:
        take(2, j)
    turn_start(1, finish(1, gather(1, last)))
    for j in order[early:]:
        last = take(2, j)
    turn_end(1)
    part = finish(2, gather(2, last))
    if 4 % nb:
        turn_start(2, part)
        turn_end(2)
        back_end(2)
    else:
        out[MAXR - 2] = masked(2, part)
    back_end(1)
    for c in sent:
        c.wait_send()


def shards(dosage, covariates, reach):
    ns, nb = lax.axis_size("sample"), lax.axis_size("variant")
    local, width = dosage.shape
    depth = -(-(covariates.shape[0] + 1) // 32) * 32
    piece = width * (depth // ROWS) // ns
    groups, rows = ns // 2, width // ns
    vmem = pltpu.VMEM
    pair = lambda n: [pltpu.SemaphoreType.DMA((n,))] * 2
    return pl.pallas_call(
        functools.partial(kernel, ns, nb),
        out_shape=jax.ShapeDtypeStruct((2 * MAXR, rows, width), BF16),
        in_specs=[pl.BlockSpec(memory_space=pltpu.HBM)] * 3,
        out_specs=pl.BlockSpec(memory_space=pltpu.VMEM),
        scratch_shapes=[
            vmem((local, width), BF16),
            vmem(covariates.shape, F32),
            pltpu.SMEM(reach.shape, jnp.int32),
            vmem((LANES, local), F32),
            vmem((6 * depth, local), BF16),
            vmem((depth, width), F32),
            vmem((ns, ROWS, piece), F32),
            vmem((ns, ROWS, piece), F32),
            vmem((ns, ROWS, piece), F32),
            vmem((ns, depth, LANES), F32),
            vmem((3, depth, width), F32),
            vmem((2, local, width), BF16),
            vmem((width, local), F32),
            vmem((width, local), BF16),
            vmem((local, width), BF16),
            vmem((ns, ROWS, width), F32),
            vmem((2 * groups, 2 * rows, width), F32),
            vmem((2 * groups, rows, width), BF16),
            vmem((2 * groups, rows, width), BF16),
            vmem((2 * groups, rows, width), BF16),
            vmem((2 * groups, rows, width), BF16),
            vmem((2, ns, rows, rows), BF16),
            vmem((2, ns, rows, rows), BF16),
            vmem((2, rows, width), BF16),
            vmem((2, rows, width), BF16),
            pltpu.SemaphoreType.DMA((3,)),
            *pair(2), *pair(ns), *pair(ns), *pair(ns), *pair(3), *pair(ns), *pair(2 * groups),
            *pair(2 * groups), *pair(2 * ns), *pair(2),
        ],
        compiler_params=pltpu.CompilerParams(
            collective_id=0, has_side_effects=True, vmem_limit_bytes=63 * 1024 * 1024
        ),
    )(dosage, covariates, reach)


def solution(mesh):
    placed = (P("sample", "variant"), P(None, "sample"), P())
    return jax.shard_map(
        shards,
        mesh=mesh,
        in_specs=placed,
        out_specs=P(None, ("variant", "sample"), None),
        check_vma=False,
    )
```

time: 53.3 us -> 46.8 us (0.88)
  Pallas kernels: 47.9 us -> 45 us
  local copies, waits for them, and re-layouts: 3.77 us -> 1.67 us
  other arithmetic: 1.44 us -> 0 us
    pallas_call x1, Pallas kernels: 47.9 us -> 45 us  [shards(): pl.pallas_call(functools.partial(kernel, ns, nb), out_shape=jax.ShapeDtyp...]
    unnamed x8 -> x1, local copies, waits for them, and re-layouts: 3.19 us -> 1.67 us
    select_n x1 -> x0, other arithmetic: 0.79 us -> none  [shards(): return jnp.where(live[:, None, None], found, jnp.zeros_like(found))]
    le x1 -> x0, other arithmetic: 0.65 us -> none  [shards(): live = distance <= reach[lax.axis_index('variant')]]
    dynamic_slice x1 -> x0, local copies, waits for them, and re-layouts: 0.58 us -> none  [shards(): live = distance <= reach[lax.axis_index('variant')]]
where the time goes in v2:
time: 46.8 us; the launch traced here: 46.7 us
  Pallas kernels  45 us (96%)
  local copies, waits for them, and re-layouts  1.67 us (4%)
    pallas_call x1, Pallas kernels, shards(): pl.pallas_call(functools.partial(kernel, ns, nb), out_shape=jax.ShapeDtyp...  45 us
    unnamed x1, local copies, waits for them, and re-layouts  1.67 us

profile of v2, /device:TPU:0, one launch (start us, length us, event | category | flops | bytes accessed | tf_op | source)
XLA Modules:
  0.0 46.7 jit_solution(5490633008284090075)
XLA Ops:
  0.0 45.0 %shard_map.37 = bf16[4,64,512]{2,1,0:T(8,128)(2,1)} custom-call(bf16[512,512]{1,0:T(8,128)(2,1)} %dosage_in.1, f32[30,512]{1,0:T(8,128)} %covariates_in.1, s32[4]{0:T(128)} %reach_in.1), custom_call_target="tpu_custom_call" | custom-call | tf_op jit(solution)/shard_map/pallas_call | solution.py:315
  45.0 1.7 %copy.5 = bf16[4,64,512]{2,1,0:T(8,128)(2,1)} copy(bf16[4,64,512]{2,1,0:T(8,128)(2,1)} %shard_map.37) | data formatting | bytes 524288

commit v3 on v2

--- a/solution.py
+++ b/solution.py
@@ -11,6 +11,7 @@
 MAXR = 2
 ROWS = 8
 LANES = 128
+VMEM_LIMIT = 63 * 1024 * 1024
 MESH = pl.DeviceIdType.MESH
 HIGHEST = lax.Precision.HIGHEST
 F32 = jnp.float32
@@ -45,32 +46,37 @@
 def eliminate(matrix, first, last):
     row_at = lax.broadcasted_iota(jnp.int32, matrix.shape, 0)
     lane_at = lax.broadcasted_iota(jnp.int32, matrix.shape, 1)
-
-    def step(k, a):
-        row = jnp.sum(jnp.where(row_at == k, a, 0.0), 0, keepdims=True)
-        column = jnp.sum(jnp.where(lane_at == k, a, 0.0), 1, keepdims=True)
-        pivot = jnp.sum(jnp.where(lane_at[:1] == k, row, 0.0), 1, keepdims=True)
-        row = jnp.where(lane_at[:1] == k, 1.0, row) / pivot
-        rest = jnp.where(lane_at == k, 0.0, a) - column * row
-        return jnp.where(row_at == k, row, rest)
-
-    return lax.fori_loop(first, last, step, matrix)
+    lane = lane_at[:1]
+    for k in range(first, last, 2):
+        one = jnp.broadcast_to(matrix[:, k : k + 1], matrix.shape)
+        two = jnp.broadcast_to(matrix[:, k + 1 : k + 2], matrix.shape)
+        a, c = one[k : k + 1], one[k + 1 : k + 2]
+        b, d = two[k : k + 1], two[k + 1 : k + 2]
+        upper = jnp.where(lane == k, 1.0, jnp.where(lane == k + 1, 0.0, matrix[k : k + 1]))
+        lower = jnp.where(lane == k, 0.0, jnp.where(lane == k + 1, 1.0, matrix[k + 1 : k + 2]))
+        ratio = c / a
+        lower = (lower - ratio * upper) / (d - ratio * b)
+        upper = (upper - b * lower) / a
+        rest = jnp.where((lane_at == k) | (lane_at == k + 1), 0.0, matrix)
+        rest = rest - one * upper - two * lower
+        matrix = jnp.where(row_at == k, upper, jnp.where(row_at == k + 1, lower, rest))
+    return matrix
 
 
 def kernel(
     ns, nb, dosage_in, covariates_in, reach_in, out,
     dosage, covariates, reach, design, terms_ref, cross, cross_out, cross_in, cross_sum, moments,
-    coefs, blocks, own_t, own_b, others, spreads, tiles, pair_out, pair_in, ring_out, ring_in,
+    blocks, own_t, own_b, spreads, tiles, pair_out, pair_in, ring_out, ring_in,
     turn_out, turn_in, back_out, back_in, load_sem,
     block_send, block_recv, cross_send, cross_recv, moment_send, moment_recv, sum_send, sum_recv,
-    coef_send, coef_recv, spread_send, spread_recv, pair_send, pair_recv, ring_send, ring_recv,
+    spread_send, spread_recv, pair_send, pair_recv, ring_send, ring_recv,
     turn_send, turn_recv, back_send, back_recv,
 ):
     s = lax.axis_index("sample")
     v = lax.axis_index("variant")
     local, width = dosage.shape
     terms = covariates.shape[0] + 1
-    depth = cross.shape[0]
+    depth = cross.shape[1]
     across = ns // (depth // ROWS)
     piece = width // across
     groups = ns // 2
@@ -101,8 +107,11 @@
     hops = sorted({1, 2, nb - 1, nb - 2})
     for j in range(1, ns):
         pl.semaphore_signal(barrier, inc=1, device_id=(sample_peer(j), v), device_id_type=MESH)
-    for j in hops:
-        pl.semaphore_signal(barrier, inc=1, device_id=(s, variant_peer(j)), device_id_type=MESH)
+    for h in hops:
+        for j in range(ns):
+            pl.semaphore_signal(
+                barrier, inc=1, device_id=(sample_peer(j), variant_peer(h)), device_id_type=MESH
+            )
 
     sent = []
 
@@ -126,7 +135,7 @@
         r, c = divmod(i, across)
         cross_out[i] = partial[r * ROWS : (r + 1) * ROWS, c * piece : (c + 1) * piece]
 
-    pl.semaphore_wait(barrier, ns - 1 + len(hops))
+    pl.semaphore_wait(barrier, ns - 1 + ns * len(hops))
     for j in range(1, ns):
         p = sample_peer(j)
         start(copy(moments.at[s], moments.at[s], moment_send.at[j], moment_recv.at[j], p, v))
@@ -152,37 +161,42 @@
         q = sample_peer(ns - j)
         copy(cross_out.at[q], cross_in.at[q], cross_send.at[j], cross_recv.at[j], q, v).wait_recv()
         total = total + cross_in[q]
-    cross_sum[s] = total
-    for j in range(1, ns):
-        p = sample_peer(j)
-        start(copy(cross_sum.at[s], cross_sum.at[s], sum_send.at[j], sum_recv.at[j], p, v))
+    cross_sum[0, s] = total
+
+    def sum_copy(k, j, slot, p):
+        return copy(cross_sum.at[0, s], cross_sum.at[k, slot], sum_send.at[k * ns + j],
+                    sum_recv.at[k * ns + j], p, variant_peer(-k))
+
+    for j in range(1, ns):
+        start(sum_copy(0, j, s, sample_peer(j)))
+    for k in (1, 2):
+        for j in range(ns):
+            start(sum_copy(k, j, s, sample_peer(j)))
     solve = eliminate(solve, depth // 4, depth)[:, :depth]
-
-    for j in range(1, ns):
-        q = sample_peer(ns - j)
-        copy(cross_sum.at[q], cross_sum.at[q], sum_send.at[j], sum_recv.at[j], q, v).wait_recv()
-    for i in range(ns):
-        r, c = divmod(i, across)
-        cross[r * ROWS : (r + 1) * ROWS, c * piece : (c + 1) * piece] = cross_sum[i]
-    coefs[0] = exact_dot(solve, cross[...], contract)
-    for k in (1, 2):
-        start(copy(coefs.at[0], coefs.at[k], coef_send.at[k], coef_recv.at[k], s, variant_peer(-k)))
     copy(dosage, blocks.at[0], block_send.at[0], block_recv.at[0], s, behind).wait_recv()
     start(copy(blocks.at[0], blocks.at[1], block_send.at[1], block_recv.at[1], s, behind))
 
-    mine = own_t[...] - fast_dot(right_terms(coefs[0], 0), terms_ref[...], ((0,), (0,)))
+    def coefficients(k):
+        for j in range(1 if k == 0 else 0, ns):
+            q = sample_peer(ns - j)
+            sum_copy(k, j, q, q).wait_recv()
+        for i in range(ns):
+            r, c = divmod(i, across)
+            cross[k, r * ROWS : (r + 1) * ROWS, c * piece : (c + 1) * piece] = cross_sum[k, i]
+        return right_terms(exact_dot(solve, cross[k], contract), 0)
+
+    mine = own_t[...] - fast_dot(coefficients(0), terms_ref[...], ((0,), (0,)))
     own_b[...] = mine.astype(BF16)
     own_t[...] = mine
     partner = group * 2 + 1 - half
     order = list(range(1, groups)) + [0]
 
     def residual(k):
-        copy(coefs.at[0], coefs.at[k], coef_send.at[k], coef_recv.at[k], s, behind).wait_recv()
         if k == 2:
             copy(blocks.at[0], blocks.at[1], block_send.at[1], block_recv.at[1], s, behind).wait_recv()
-        fitted = fast_dot(terms_ref[...], right_terms(coefs[k], 0), ((0,), (0,)))
+        fitted = fast_dot(terms_ref[...], coefficients(k), ((0,), (0,)))
         theirs = blocks[k - 1].astype(F32) - fitted
-        others[...] = theirs.astype(BF16)
+        tiles[k - 1] = fast_dot(own_b[...], theirs.astype(BF16), contract)
         spreads[s, k : k + 1] = jnp.sum(theirs * theirs, 0, keepdims=True)
 
     def slot(k, j):
@@ -200,15 +214,16 @@
     def give(k, j):
         i = slot(k, j)
         g = lax.rem(group + j, groups)
-        lhs = own_b[pl.ds(pl.multiple_of(g * 2 * rows, 2 * rows), 2 * rows)]
-        tiles[i] = fast_dot(lhs, others[...], contract)
-        pair_out[i] = tiles[i, pl.ds(pl.multiple_of((1 - half) * rows, rows), rows)].astype(BF16)
+        at = pl.multiple_of((g * 2 + 1 - half) * rows, rows)
+        pair_out[i] = tiles[k - 1, pl.ds(at, rows)].astype(BF16)
         start(pair_copy(k, j))
 
     def take(k, j):
         i = slot(k, j)
         pair_copy(k, j).wait_recv()
-        summed = tiles[i, pl.ds(pl.multiple_of(half * rows, rows), rows)] + pair_in[i].astype(F32)
+        g = lax.rem(group + j, groups)
+        at = pl.multiple_of((g * 2 + half) * rows, rows)
+        summed = tiles[k - 1, pl.ds(at, rows)] + pair_in[i].astype(F32)
         if j:
             ring_out[i] = summed.astype(BF16)
             start(ring_copy(k, j))
@@ -323,18 +338,16 @@
             pltpu.SMEM(reach.shape, jnp.int32),
             vmem((LANES, local), F32),
             vmem((6 * depth, local), BF16),
-            vmem((depth, width), F32),
+            vmem((3, depth, width), F32),
             vmem((ns, ROWS, piece), F32),
             vmem((ns, ROWS, piece), F32),
-            vmem((ns, ROWS, piece), F32),
+            vmem((3, ns, ROWS, piece), F32),
             vmem((ns, depth, LANES), F32),
-            vmem((3, depth, width), F32),
             vmem((2, local, width), BF16),
             vmem((width, local), F32),
             vmem((width, local), BF16),
-            vmem((local, width), BF16),
             vmem((ns, ROWS, width), F32),
-            vmem((2 * groups, 2 * rows, width), F32),
+            vmem((2, width, width), F32),
             vmem((2 * groups, rows, width), BF16),
             vmem((2 * groups, rows, width), BF16),
             vmem((2 * groups, rows, width), BF16),
@@ -344,11 +357,11 @@
             vmem((2, rows, width), BF16),
             vmem((2, rows, width), BF16),
             pltpu.SemaphoreType.DMA((3,)),
-            *pair(2), *pair(ns), *pair(ns), *pair(ns), *pair(3), *pair(ns), *pair(2 * groups),
+            *pair(2), *pair(ns), *pair(ns), *pair(3 * ns), *pair(ns), *pair(2 * groups),
             *pair(2 * groups), *pair(2 * ns), *pair(2),
         ],
         compiler_params=pltpu.CompilerParams(
-            collective_id=0, has_side_effects=True, vmem_limit_bytes=63 * 1024 * 1024
+            collective_id=0, has_side_effects=True, vmem_limit_bytes=VMEM_LIMIT
         ),
     )(dosage, covariates, reach)
 

time: 46.8 us -> 49.3 us (1.053)
  Pallas kernels: 45 us -> 47.5 us
    pallas_call x1, Pallas kernels: 45 us -> 47.5 us  [shards(): pl.pallas_call(functools.partial(kernel, ns, nb), out_shape=jax.ShapeDtyp...]
where the time goes in v3:
time: 49.3 us; the launch traced here: 49.1 us
  Pallas kernels  47.5 us (96%)
  local copies, waits for them, and re-layouts  1.67 us (3%)
    pallas_call x1, Pallas kernels, shards(): pl.pallas_call(functools.partial(kernel, ns, nb), out_shape=jax.ShapeDtyp...  47.5 us
    unnamed x1, local copies, waits for them, and re-layouts  1.67 us

profile of v3, /device:TPU:0, one launch (start us, length us, event | category | flops | bytes accessed | tf_op | source)
XLA Modules:
  0.0 49.1 jit_solution(4465233773514456930)
XLA Ops:
  0.0 47.5 %shard_map.37 = bf16[4,64,512]{2,1,0:T(8,128)(2,1)} custom-call(bf16[512,512]{1,0:T(8,128)(2,1)} %dosage_in.1, f32[30,512]{1,0:T(8,128)} %covariates_in.1, s32[4]{0:T(128)} %reach_in.1), custom_call_target="tpu_custom_call" | custom-call | tf_op jit(solution)/shard_map/pallas_call | solution.py:330
  47.5 1.7 %copy.5 = bf16[4,64,512]{2,1,0:T(8,128)(2,1)} copy(bf16[4,64,512]{2,1,0:T(8,128)(2,1)} %shard_map.37) | data formatting | bytes 524288

commit v4 on v3

--- a/solution.py
+++ b/solution.py
@@ -65,10 +65,10 @@
 
 def kernel(
     ns, nb, dosage_in, covariates_in, reach_in, out,
-    dosage, covariates, reach, design, terms_ref, cross, cross_out, cross_in, cross_sum, moments,
+    dosage, covariates, reach, design, terms_ref, cross, cross_out, cross_in, cross_sum, coefs,
     blocks, own_t, own_b, spreads, tiles, pair_out, pair_in, ring_out, ring_in,
     turn_out, turn_in, back_out, back_in, load_sem,
-    block_send, block_recv, cross_send, cross_recv, moment_send, moment_recv, sum_send, sum_recv,
+    block_send, block_recv, cross_send, cross_recv, sum_send, sum_recv, coef_send, coef_recv,
     spread_send, spread_recv, pair_send, pair_recv, ring_send, ring_recv,
     turn_send, turn_recv, back_send, back_recv,
 ):
@@ -76,7 +76,7 @@
     v = lax.axis_index("variant")
     local, width = dosage.shape
     terms = covariates.shape[0] + 1
-    depth = cross.shape[1]
+    depth = cross.shape[0]
     across = ns // (depth // ROWS)
     piece = width // across
     groups = ns // 2
@@ -107,13 +107,15 @@
     hops = sorted({1, 2, nb - 1, nb - 2})
     for j in range(1, ns):
         pl.semaphore_signal(barrier, inc=1, device_id=(sample_peer(j), v), device_id_type=MESH)
-    for h in hops:
-        for j in range(ns):
-            pl.semaphore_signal(
-                barrier, inc=1, device_id=(sample_peer(j), variant_peer(h)), device_id_type=MESH
-            )
+    for j in hops:
+        pl.semaphore_signal(barrier, inc=1, device_id=(s, variant_peer(j)), device_id_type=MESH)
 
     sent = []
+
+    def flush(count):
+        for c in sent[:count]:
+            c.wait_send()
+        del sent[:count]
 
     def start(c):
         c.start()
@@ -126,78 +128,79 @@
     design[1:terms] = covariates[...]
     full = design[0:depth]
     high, middle, low = pieces(full)
-    moments[s] = exact_dot(full, design[...], ((1,), (1,)))
+    moment = exact_dot(full, design[...], ((1,), (1,)))[:, :depth]
+    packed = jnp.concatenate([moment[r : r + ROWS] for r in range(0, depth, ROWS)], 1)
     load_dosage.wait()
     genotype = dosage[...]
     partial = fast_dot(jnp.concatenate([high, middle, low], 0), genotype, contract)
     partial = partial[:depth] + (partial[depth : 2 * depth] + partial[2 * depth :])
     for i in range(ns):
         r, c = divmod(i, across)
-        cross_out[i] = partial[r * ROWS : (r + 1) * ROWS, c * piece : (c + 1) * piece]
-
-    pl.semaphore_wait(barrier, ns - 1 + ns * len(hops))
-    for j in range(1, ns):
-        p = sample_peer(j)
-        start(copy(moments.at[s], moments.at[s], moment_send.at[j], moment_recv.at[j], p, v))
-        start(copy(cross_out.at[p], cross_in.at[s], cross_send.at[j], cross_recv.at[j], p, v))
+        cross_out[i, :, :piece] = partial[r * ROWS : (r + 1) * ROWS, c * piece : (c + 1) * piece]
+        cross_out[i, :, piece:] = packed
+
+    pl.semaphore_wait(barrier, ns - 1 + len(hops))
     behind = variant_peer(-1)
     start(copy(dosage, blocks.at[0], block_send.at[0], block_recv.at[0], s, behind))
-
+    for j in range(1, ns):
+        p = sample_peer(j)
+        start(copy(cross_out.at[p], cross_in.at[s], cross_send.at[j], cross_recv.at[j], p, v))
     terms_ref[...] = left_terms(full, 0)
     own_t[...] = genotype.astype(F32).T
 
-    moment = moments[s]
+    total = cross_out[s]
     for j in range(1, ns):
         q = sample_peer(ns - j)
-        copy(moments.at[q], moments.at[q], moment_send.at[j], moment_recv.at[j], q, v).wait_recv()
-        moment = moment + moments[q]
+        copy(cross_out.at[q], cross_in.at[q], cross_send.at[j], cross_recv.at[j], q, v).wait_recv()
+        total = total + cross_in[q]
+    cross_sum[s] = total[:, :piece]
+
+    def sum_copy(j, slot, p):
+        return copy(cross_sum.at[s], cross_sum.at[slot], sum_send.at[j], sum_recv.at[j], p, v)
+
+    for j in range(1, ns):
+        start(sum_copy(j, s, sample_peer(j)))
+    packed = total[:, piece:]
+    shares = [packed[:, r * depth : (r + 1) * depth] for r in range(depth // ROWS)]
+    moment = jnp.concatenate(shares, 0)
     row_at = lax.broadcasted_iota(jnp.int32, moment.shape, 0)
     lane_at = lax.broadcasted_iota(jnp.int32, moment.shape, 1)
     moment = jnp.where((row_at == lane_at) & (row_at >= terms), 1.0, moment)
-    solve = eliminate(moment, 0, depth // 4)
-
-    total = cross_out[s]
+    solve = eliminate(moment, 0, depth)
     for j in range(1, ns):
         q = sample_peer(ns - j)
-        copy(cross_out.at[q], cross_in.at[q], cross_send.at[j], cross_recv.at[j], q, v).wait_recv()
-        total = total + cross_in[q]
-    cross_sum[0, s] = total
-
-    def sum_copy(k, j, slot, p):
-        return copy(cross_sum.at[0, s], cross_sum.at[k, slot], sum_send.at[k * ns + j],
-                    sum_recv.at[k * ns + j], p, variant_peer(-k))
-
-    for j in range(1, ns):
-        start(sum_copy(0, j, s, sample_peer(j)))
+        sum_copy(j, q, q).wait_recv()
+    for i in range(ns):
+        r, c = divmod(i, across)
+        cross[r * ROWS : (r + 1) * ROWS, c * piece : (c + 1) * piece] = cross_sum[i]
+    coefs[0] = exact_dot(solve, cross[...], contract)
+
+    def coef_copy(k):
+        return copy(coefs.at[0], coefs.at[k], coef_send.at[k], coef_recv.at[k], s, variant_peer(-k))
+
     for k in (1, 2):
-        for j in range(ns):
-            start(sum_copy(k, j, s, sample_peer(j)))
-    solve = eliminate(solve, depth // 4, depth)[:, :depth]
+        start(coef_copy(k))
     copy(dosage, blocks.at[0], block_send.at[0], block_recv.at[0], s, behind).wait_recv()
     start(copy(blocks.at[0], blocks.at[1], block_send.at[1], block_recv.at[1], s, behind))
 
-    def coefficients(k):
-        for j in range(1 if k == 0 else 0, ns):
-            q = sample_peer(ns - j)
-            sum_copy(k, j, q, q).wait_recv()
-        for i in range(ns):
-            r, c = divmod(i, across)
-            cross[k, r * ROWS : (r + 1) * ROWS, c * piece : (c + 1) * piece] = cross_sum[k, i]
-        return right_terms(exact_dot(solve, cross[k], contract), 0)
-
-    mine = own_t[...] - fast_dot(coefficients(0), terms_ref[...], ((0,), (0,)))
+    mine = own_t[...] - fast_dot(right_terms(coefs[0], 0), terms_ref[...], ((0,), (0,)))
     own_b[...] = mine.astype(BF16)
     own_t[...] = mine
     partner = group * 2 + 1 - half
     order = list(range(1, groups)) + [0]
 
+    def store_spread(k, values):
+        spreads[s, k : k + 1] = values[:, : width // 2]
+        spreads[s, k + 3 : k + 4] = values[:, width // 2 :]
+
     def residual(k):
+        coef_copy(k).wait_recv()
         if k == 2:
             copy(blocks.at[0], blocks.at[1], block_send.at[1], block_recv.at[1], s, behind).wait_recv()
-        fitted = fast_dot(terms_ref[...], coefficients(k), ((0,), (0,)))
+        fitted = fast_dot(terms_ref[...], right_terms(coefs[k], 0), ((0,), (0,)))
         theirs = blocks[k - 1].astype(F32) - fitted
         tiles[k - 1] = fast_dot(own_b[...], theirs.astype(BF16), contract)
-        spreads[s, k : k + 1] = jnp.sum(theirs * theirs, 0, keepdims=True)
+        store_spread(k, jnp.sum(theirs * theirs, 0, keepdims=True))
 
     def slot(k, j):
         return (k - 1) * groups + j
@@ -236,13 +239,15 @@
         return summed
 
     residual(1)
+    early_sends = len(sent)
     for j in order:
         give(1, j)
     column = jnp.sum(mine * mine, 1, keepdims=True)
-    spreads[s, 0:1] = jnp.broadcast_to(column, (width, LANES)).T[0:1]
-    spreads[s, 3:ROWS] = jnp.zeros((ROWS - 3, width), F32)
+    store_spread(0, jnp.broadcast_to(column, (width, LANES)).T[0:1])
+    spreads[s, 6:ROWS] = jnp.zeros((ROWS - 6, width // 2), F32)
     for j in order[:1]:
         take(1, j)
+    flush(early_sends)
     residual(2)
     for j in range(1, ns):
         p = sample_peer(j)
@@ -252,12 +257,13 @@
         if n:
             last = take(1, j)
 
+    middle_sends = len(sent)
     spread = spreads[s]
     for j in range(1, ns):
         q = sample_peer(ns - j)
         copy(spreads.at[q], spreads.at[q], spread_send.at[j], spread_recv.at[j], q, v).wait_recv()
         spread = spread + spreads[q]
-    scale = jnp.sqrt(samples / spread[0:3])
+    scale = jnp.sqrt(samples / jnp.concatenate([spread[0:3], spread[3:6]], 1))
     chosen = lax.broadcasted_iota(jnp.int32, (rows, width), 1) == (
         lax.broadcasted_iota(jnp.int32, (rows, width), 0) + s * rows
     )
@@ -306,6 +312,7 @@
     turn_start(1, finish(1, gather(1, last)))
     for j in order[early:]:
         last = take(2, j)
+    flush(middle_sends)
     turn_end(1)
     part = finish(2, gather(2, last))
     if 4 % nb:
@@ -315,8 +322,7 @@
     else:
         out[MAXR - 2] = masked(2, part)
     back_end(1)
-    for c in sent:
-        c.wait_send()
+    flush(len(sent))
 
 
 def shards(dosage, covariates, reach):
@@ -338,15 +344,15 @@
             pltpu.SMEM(reach.shape, jnp.int32),
             vmem((LANES, local), F32),
             vmem((6 * depth, local), BF16),
+            vmem((depth, width), F32),
+            vmem((ns, ROWS, piece + LANES), F32),
+            vmem((ns, ROWS, piece + LANES), F32),
+            vmem((ns, ROWS, piece), F32),
             vmem((3, depth, width), F32),
-            vmem((ns, ROWS, piece), F32),
-            vmem((ns, ROWS, piece), F32),
-            vmem((3, ns, ROWS, piece), F32),
-            vmem((ns, depth, LANES), F32),
             vmem((2, local, width), BF16),
             vmem((width, local), F32),
             vmem((width, local), BF16),
-            vmem((ns, ROWS, width), F32),
+            vmem((ns, ROWS, width // 2), F32),
             vmem((2, width, width), F32),
             vmem((2 * groups, rows, width), BF16),
             vmem((2 * groups, rows, width), BF16),
@@ -357,7 +363,7 @@
             vmem((2, rows, width), BF16),
             vmem((2, rows, width), BF16),
             pltpu.SemaphoreType.DMA((3,)),
-            *pair(2), *pair(ns), *pair(ns), *pair(3 * ns), *pair(ns), *pair(2 * groups),
+            *pair(2), *pair(ns), *pair(ns), *pair(3), *pair(ns), *pair(2 * groups),
             *pair(2 * groups), *pair(2 * ns), *pair(2),
         ],
         compiler_params=pltpu.CompilerParams(

time: 49.3 us -> 45.1 us (0.915)
  Pallas kernels: 47.5 us -> 43.3 us
    pallas_call x1, Pallas kernels: 47.5 us -> 43.3 us  [shards(): pl.pallas_call(functools.partial(kernel, ns, nb), out_shape=jax.ShapeDtyp...]
where the time goes in v4:
time: 45.1 us; the launch traced here: 45 us
  Pallas kernels  43.3 us (96%)
  local copies, waits for them, and re-layouts  1.67 us (4%)
    pallas_call x1, Pallas kernels, shards(): pl.pallas_call(functools.partial(kernel, ns, nb), out_shape=jax.ShapeDtyp...  43.3 us
    unnamed x1, local copies, waits for them, and re-layouts  1.67 us

profile of v4, /device:TPU:0, one launch (start us, length us, event | category | flops | bytes accessed | tf_op | source)
XLA Modules:
  0.0 45.0 jit_solution(6844690859437006889)
XLA Ops:
  0.0 43.3 %shard_map.37 = bf16[4,64,512]{2,1,0:T(8,128)(2,1)} custom-call(bf16[512,512]{1,0:T(8,128)(2,1)} %dosage_in.1, f32[30,512]{1,0:T(8,128)} %covariates_in.1, s32[4]{0:T(128)} %reach_in.1), custom_call_target="tpu_custom_call" | custom-call | tf_op jit(solution)/shard_map/pallas_call | solution.py:336
  43.3 1.7 %copy.5 = bf16[4,64,512]{2,1,0:T(8,128)(2,1)} copy(bf16[4,64,512]{2,1,0:T(8,128)(2,1)} %shard_map.37) | data formatting | bytes 524288

commit v5 on v4

--- a/solution.py
+++ b/solution.py
@@ -141,10 +141,18 @@
 
     pl.semaphore_wait(barrier, ns - 1 + len(hops))
     behind = variant_peer(-1)
-    start(copy(dosage, blocks.at[0], block_send.at[0], block_recv.at[0], s, behind))
     for j in range(1, ns):
         p = sample_peer(j)
         start(copy(cross_out.at[p], cross_in.at[s], cross_send.at[j], cross_recv.at[j], p, v))
+
+    def block_copy(k, part):
+        at = pl.ds(part * (local // 2), local // 2)
+        src = dosage if k == 1 else blocks.at[0]
+        i = (k - 1) * 2 + part
+        return copy(src.at[at], blocks.at[k - 1, at], block_send.at[i], block_recv.at[i], s, behind)
+
+    for part in (0, 1):
+        start(block_copy(1, part))
     terms_ref[...] = left_terms(full, 0)
     own_t[...] = genotype.astype(F32).T
 
@@ -167,6 +175,8 @@
     lane_at = lax.broadcasted_iota(jnp.int32, moment.shape, 1)
     moment = jnp.where((row_at == lane_at) & (row_at >= terms), 1.0, moment)
     solve = eliminate(moment, 0, depth)
+    block_copy(1, 0).wait_recv()
+    start(block_copy(2, 0))
     for j in range(1, ns):
         q = sample_peer(ns - j)
         sum_copy(j, q, q).wait_recv()
@@ -180,8 +190,8 @@
 
     for k in (1, 2):
         start(coef_copy(k))
-    copy(dosage, blocks.at[0], block_send.at[0], block_recv.at[0], s, behind).wait_recv()
-    start(copy(blocks.at[0], blocks.at[1], block_send.at[1], block_recv.at[1], s, behind))
+    block_copy(1, 1).wait_recv()
+    start(block_copy(2, 1))
 
     mine = own_t[...] - fast_dot(right_terms(coefs[0], 0), terms_ref[...], ((0,), (0,)))
     own_b[...] = mine.astype(BF16)
@@ -196,7 +206,8 @@
     def residual(k):
         coef_copy(k).wait_recv()
         if k == 2:
-            copy(blocks.at[0], blocks.at[1], block_send.at[1], block_recv.at[1], s, behind).wait_recv()
+            for part in (0, 1):
+                block_copy(2, part).wait_recv()
         fitted = fast_dot(terms_ref[...], right_terms(coefs[k], 0), ((0,), (0,)))
         theirs = blocks[k - 1].astype(F32) - fitted
         tiles[k - 1] = fast_dot(own_b[...], theirs.astype(BF16), contract)
@@ -363,7 +374,7 @@
             vmem((2, rows, width), BF16),
             vmem((2, rows, width), BF16),
             pltpu.SemaphoreType.DMA((3,)),
-            *pair(2), *pair(ns), *pair(ns), *pair(3), *pair(ns), *pair(2 * groups),
+            *pair(4), *pair(ns), *pair(ns), *pair(3), *pair(ns), *pair(2 * groups),
             *pair(2 * groups), *pair(2 * ns), *pair(2),
         ],
         compiler_params=pltpu.CompilerParams(

time: 45.1 us -> 43.8 us (0.971)
  Pallas kernels: 43.3 us -> 42 us
    pallas_call x1, Pallas kernels: 43.3 us -> 42 us  [shards(): pl.pallas_call(functools.partial(kernel, ns, nb), out_shape=jax.ShapeDtyp...]
where the time goes in v5:
time: 43.8 us; the launch traced here: 43.7 us
  Pallas kernels  42 us (96%)
  local copies, waits for them, and re-layouts  1.67 us (4%)
    pallas_call x1, Pallas kernels, shards(): pl.pallas_call(functools.partial(kernel, ns, nb), out_shape=jax.ShapeDtyp...  42 us
    unnamed x1, local copies, waits for them, and re-layouts  1.67 us

profile of v5, /device:TPU:0, one launch (start us, length us, event | category | flops | bytes accessed | tf_op | source)
XLA Modules:
  0.0 43.7 jit_solution(7543302854625881514)
XLA Ops:
  0.0 42.0 %shard_map.37 = bf16[4,64,512]{2,1,0:T(8,128)(2,1)} custom-call(bf16[512,512]{1,0:T(8,128)(2,1)} %dosage_in.1, f32[30,512]{1,0:T(8,128)} %covariates_in.1, s32[4]{0:T(128)} %reach_in.1), custom_call_target="tpu_custom_call" | custom-call | tf_op jit(solution)/shard_map/pallas_call | solution.py:347
  42.0 1.7 %copy.5 = bf16[4,64,512]{2,1,0:T(8,128)(2,1)} copy(bf16[4,64,512]{2,1,0:T(8,128)(2,1)} %shard_map.37) | data formatting | bytes 524288

commit v6 on v5

--- a/solution.py
+++ b/solution.py
@@ -183,7 +183,7 @@
     for i in range(ns):
         r, c = divmod(i, across)
         cross[r * ROWS : (r + 1) * ROWS, c * piece : (c + 1) * piece] = cross_sum[i]
-    coefs[0] = exact_dot(solve, cross[...], contract)
+    coefs[0] = fast_dot(left_terms(solve, 1), right_terms(cross[...], 0), contract)
 
     def coef_copy(k):
         return copy(coefs.at[0], coefs.at[k], coef_send.at[k], coef_recv.at[k], s, variant_peer(-k))

time: 43.8 us -> 43.3 us (0.989)
  Pallas kernels: 42 us -> 41.5 us
    pallas_call x1, Pallas kernels: 42 us -> 41.5 us  [shards(): pl.pallas_call(functools.partial(kernel, ns, nb), out_shape=jax.ShapeDtyp...]
where the time goes in v6:
time: 43.3 us; the launch traced here: 43.2 us
  Pallas kernels  41.5 us (96%)
  local copies, waits for them, and re-layouts  1.67 us (4%)
    pallas_call x1, Pallas kernels, shards(): pl.pallas_call(functools.partial(kernel, ns, nb), out_shape=jax.ShapeDtyp...  41.5 us
    unnamed x1, local copies, waits for them, and re-layouts  1.67 us

profile of v6, /device:TPU:0, one launch (start us, length us, event | category | flops | bytes accessed | tf_op | source)
XLA Modules:
  0.0 43.2 jit_solution(37733652726745968)
XLA Ops:
  0.0 41.5 %shard_map.37 = bf16[4,64,512]{2,1,0:T(8,128)(2,1)} custom-call(bf16[512,512]{1,0:T(8,128)(2,1)} %dosage_in.1, f32[30,512]{1,0:T(8,128)} %covariates_in.1, s32[4]{0:T(128)} %reach_in.1), custom_call_target="tpu_custom_call" | custom-call | tf_op jit(solution)/shard_map/pallas_call | solution.py:347
  41.5 1.7 %copy.5 = bf16[4,64,512]{2,1,0:T(8,128)(2,1)} copy(bf16[4,64,512]{2,1,0:T(8,128)(2,1)} %shard_map.37) | data formatting | bytes 524288
